TPU v7x, 32 devices: a whole 2x2x4 slice. The times are simulated.
32 devices in a mesh: ctx: 16 (over z, y, x), head: 2 (over core).
Axes of the slice: x: 2, y: 2, z: 4, core: 2. Of those that a mesh axis runs over, the one named last changes fastest.
Arguments:
- query: bfloat16 [4096, 8192], P(('ctx', 'head')), may hold values from -20 to 20
- key: bfloat16 [4096, 1024], P(('ctx', 'head')), may hold values from -6 to 6
- value: bfloat16 [4096, 1024], P(('ctx', 'head')), may hold values from -6 to 6
- doc_lengths: int32 [4], replicated, may hold values from 256 to 2048, as said below
- block_place: int32 [256], replicated, may hold values from 0 to 255, as said below
Outputs:
- attended: bfloat16 [4096, 8192], P('ctx', 'head')
Inputs may be any that keep to these rules, and one draw needn't show every extreme that they name: `doc_lengths`: 4 lengths that sum to 4096; the longest is exactly 2048 and the shortest exactly 256. `block_place`: A permutation of the blocks. The 8 blocks of one loading device (one index of ctx+head, ctx slowest) go to distinct context shards; context shard s holds packed blocks s * 16 to (s + 1) * 16 - 1.
All inputs are finite; a program needn't handle non-finite values.
Results may differ from a plain program's by a relative error of at most 0.0028.
Values may be sent and summed in bfloat16 or wider, within the bound.
No kernel may reach another device: no remote copies, remote signals or barrier semaphores. Data moves between devices by JAX's collectives and lax.ppermute only.
A program may use at most 192 MiB of HBM per device.

v0:
```python
import jax
import jax.numpy as jnp
from jax import lax
from jax.sharding import PartitionSpec as P

HD = 128
SPAN = 8


def shifted(block, axis, distance):
    devices = range(lax.axis_size(axis))
    route = [(i - distance, i) for i in devices if i - distance in devices]
    return lax.ppermute(block, axis, route)


def doc_starts(positions, doc_lengths):
    doc_ends = jnp.cumsum(doc_lengths)
    before = jnp.where(positions[:, None] >= doc_ends[None, :], doc_lengths[None, :], 0)
    return jnp.sum(before, axis=1)


def body(query, key, value, doc_lengths, block_place):
    ctx_count = lax.axis_size("ctx")
    head_count = lax.axis_size("head")
    loaded_rows = query.shape[0]
    shard_rows = loaded_rows * head_count
    block_rows = shard_rows // ctx_count
    per_loader = loaded_rows // block_rows
    shard_blocks = shard_rows // block_rows
    shard_index = lax.axis_index("ctx")
    group_index = lax.axis_index("head")
    loader = shard_index * head_count + group_index
    assigned = lax.dynamic_slice_in_dim(block_place, loader * per_loader, per_loader)
    targets = assigned // shard_blocks
    matched = targets[None, :] == jnp.arange(ctx_count, dtype=jnp.int32)[:, None]
    sources = jnp.sum(
        jnp.where(matched, jnp.arange(per_loader, dtype=jnp.int32)[None, :], 0), axis=1
    )
    filled = jnp.any(matched, axis=1)

    def outgoing(loaded):
        blocks = loaded.reshape(per_loader, block_rows, loaded.shape[1])
        picked = jnp.take(blocks, sources, axis=0)
        return jnp.where(filled[:, None, None], picked, jnp.zeros_like(picked))

    sending = (outgoing(query), outgoing(key), outgoing(value))
    arrived = (
        lax.all_to_all(
            lax.all_to_all(sending[0], "ctx", split_axis=0, concat_axis=0, tiled=True),
            "head",
            split_axis=2,
            concat_axis=1,
            tiled=True,
        ),
        lax.all_to_all(
            lax.all_to_all(sending[1], "ctx", split_axis=0, concat_axis=0, tiled=True),
            "head",
            split_axis=2,
            concat_axis=1,
            tiled=True,
        ),
        lax.all_to_all(
            lax.all_to_all(sending[2], "ctx", split_axis=0, concat_axis=0, tiled=True),
            "head",
            split_axis=2,
            concat_axis=1,
            tiled=True,
        ),
    )
    inverse = jnp.argsort(block_place)
    wanted = lax.dynamic_slice_in_dim(inverse, shard_index * shard_blocks, shard_blocks)
    source_slot = wanted // per_loader

    def incoming(received):
        blocks = received.reshape(ctx_count * head_count, block_rows, received.shape[2])
        return jnp.take(blocks, source_slot, axis=0).reshape(shard_rows, received.shape[2])

    query_local = incoming(arrived[0])
    key_local = incoming(arrived[1])
    value_local = incoming(arrived[2])
    own_pair = jnp.stack([key_local, value_local])
    earlier = [shifted(own_pair, "ctx", offset) for offset in range(SPAN, 0, -1)]
    window = jnp.concatenate(earlier + [own_pair], axis=1)
    tile_rows = min(256, shard_rows)
    tile_count = window.shape[1] // tile_rows
    key_tiles = window[0].reshape(tile_count, tile_rows, window.shape[2])
    value_tiles = window[1].reshape(tile_count, tile_rows, window.shape[2])
    key_heads = key_local.shape[1] // HD
    query_groups = query_local.shape[1] // key_local.shape[1]
    query_rows = shard_index * shard_rows + jnp.arange(shard_rows, dtype=jnp.int32)
    doc_start = doc_starts(query_rows, doc_lengths)
    window_start = (shard_index - SPAN) * shard_rows
    queries = query_local.reshape(shard_rows, key_heads, query_groups, HD)
    score_scale = HD ** (-0.5)

    def absorb(running, tile_data):
        running_max, running_sum, numerator = running
        tile_keys, tile_values, tile_index = tile_data
        tile_start = window_start + tile_index * tile_rows
        key_rows = tile_start + jnp.arange(tile_rows, dtype=jnp.int32)
        visible = (key_rows[None, :] >= doc_start[:, None]) & (
            key_rows[None, :] <= query_rows[:, None]
        )
        visible = visible[:, None, None, :]
        keys_split = tile_keys.reshape(tile_rows, key_heads, HD)
        values_split = tile_values.reshape(tile_rows, key_heads, HD)
        scores = (
            jnp.einsum("tkgd,skd->tkgs", queries, keys_split, preferred_element_type=jnp.float32)
            * score_scale
        )
        scores = jnp.where(visible, scores, -1e30)
        new_max = jnp.maximum(running_max, jnp.max(scores, axis=-1))
        weights = jnp.where(visible, jnp.exp(scores - new_max[..., None]), 0.0)
        factor = jnp.exp(running_max - new_max)
        running_sum = running_sum * factor + jnp.sum(weights, axis=-1)
        product = jnp.einsum(
            "tkgs,skd->tkgd",
            weights.astype(jnp.bfloat16),
            values_split,
            preferred_element_type=jnp.float32,
        )
        numerator = numerator * factor[..., None] + product
        return (new_max, running_sum, numerator)

    def advance(running, tile_data):
        running = absorb(running, tile_data)
        return (running, None)

    initial = (
        jnp.full((shard_rows, key_heads, query_groups), -1e30, jnp.float32),
        jnp.zeros((shard_rows, key_heads, query_groups), jnp.float32),
        jnp.zeros((shard_rows, key_heads, query_groups, HD), jnp.float32),
    )
    final, unused = lax.scan(
        advance, initial, (key_tiles, value_tiles, jnp.arange(tile_count, dtype=jnp.int32))
    )
    result = (final[2] / final[1][..., None]).astype(jnp.bfloat16)
    return result.reshape(shard_rows, query_local.shape[1])


def solution(mesh):
    placed = (
        P(("ctx", "head"), None),
        P(("ctx", "head"), None),
        P(("ctx", "head"), None),
        P(),
        P(),
    )
    return jax.shard_map(
        body, mesh=mesh, in_specs=placed, out_specs=P("ctx", "head"), check_vma=False
    )
```

profile of v0, /device:TPU:14, one launch (start us, length us, event | category | flops | bytes accessed | tf_op | source)
XLA Modules:
  0.0 688.8 jit_solution(2126670612861438360)
XLA Ops:
  15.3 10.2 %all-to-all-done.2 = bf16[16,16,1024]{2,1,0:T(8,128)(2,1)S(1)} async-done(((bf16[16,16,1024]{2,1,0:T(8,128)(2,1)}), bf16[16,16,1024]{2,1,0:T(8,128)(2,1)S(1)}, u32[]{:S(2)}, u32[]{:S(2)}) %all-to-all-start.2) | async-done | bytes 524320 | tf_op jit(solution)/shard_map/all_to_all | solution.py:63
  116.5 107.0 %collective-permute-done = bf16[2,256,512]{2,1,0:T(8,128)(2,1)} collective-permute-done((bf16[2,256,512]{2,1,0:T(8,128)(2,1)S(1)}, bf16[2,256,512]{2,1,0:T(8,128)(2,1)}, u32[]{:S(2)}, u32[]{:S(2)}) %collective-permute-start) | collective-permute-done | bytes 524320 | tf_op jit(solution)/shard_map/ppermute | solution.py:13
  236.7 17.9 %collective-permute-done.2 = bf16[2,256,512]{2,1,0:T(8,128)(2,1)S(1)} collective-permute-done((bf16[2,256,512]{2,1,0:T(8,128)(2,1)S(1)}, bf16[2,256,512]{2,1,0:T(8,128)(2,1)S(1)}, u32[]{:S(2)}, u32[]{:S(2)}) %collective-permute-start.2) | collective-permute-done | bytes 524320 | tf_op jit(solution)/shard_map/ppermute | solution.py:13
  256.7 13.9 %collective-permute-done.3 = bf16[2,256,512]{2,1,0:T(8,128)(2,1)S(1)} collective-permute-done((bf16[2,256,512]{2,1,0:T(8,128)(2,1)S(1)}, bf16[2,256,512]{2,1,0:T(8,128)(2,1)S(1)}, u32[]{:S(2)}, u32[]{:S(2)}) %collective-permute-start.3) | collective-permute-done | bytes 524320 | tf_op jit(solution)/shard_map/ppermute | solution.py:13
  270.7 11.2 %collective-permute-done.4 = bf16[2,256,512]{2,1,0:T(8,128)(2,1)S(1)} collective-permute-done((bf16[2,256,512]{2,1,0:T(8,128)(2,1)S(1)}, bf16[2,256,512]{2,1,0:T(8,128)(2,1)S(1)}, u32[]{:S(2)}, u32[]{:S(2)}) %collective-permute-start.4) | collective-permute-done | bytes 524320 | tf_op jit(solution)/shard_map/ppermute | solution.py:13
  281.9 11.2 %collective-permute-done.5 = bf16[2,256,512]{2,1,0:T(8,128)(2,1)S(1)} collective-permute-done((bf16[2,256,512]{2,1,0:T(8,128)(2,1)S(1)}, bf16[2,256,512]{2,1,0:T(8,128)(2,1)S(1)}, u32[]{:S(2)}, u32[]{:S(2)}) %collective-permute-start.5) | collective-permute-done | bytes 524320 | tf_op jit(solution)/shard_map/ppermute | solution.py:13
  293.1 11.2 %collective-permute-done.6 = bf16[2,256,512]{2,1,0:T(8,128)(2,1)S(1)} collective-permute-done((bf16[2,256,512]{2,1,0:T(8,128)(2,1)S(1)}, bf16[2,256,512]{2,1,0:T(8,128)(2,1)S(1)}, u32[]{:S(2)}, u32[]{:S(2)}) %collective-permute-start.6) | collective-permute-done | bytes 524320 | tf_op jit(solution)/shard_map/ppermute | solution.py:13
  304.4 10.1 %collective-permute-done.7 = bf16[2,256,512]{2,1,0:T(8,128)(2,1)S(1)} collective-permute-done((bf16[2,256,512]{2,1,0:T(8,128)(2,1)S(1)}, bf16[2,256,512]{2,1,0:T(8,128)(2,1)S(1)}, u32[]{:S(2)}, u32[]{:S(2)}) %collective-permute-start.7) | collective-permute-done | bytes 524320 | tf_op jit(solution)/shard_map/ppermute | solution.py:13
  317.0 27.6 %copy.43 = bf16[16,16,8192]{1,0,2:T(8,128)(2,1)} copy(bf16[16,16,8192]{2,1,0:T(8,128)(2,1)} %all-to-all-done.4) | data formatting | bytes 8388608 | tf_op jit(solution)/shard_map/all_to_all | solution.py:49
  344.6 29.1 %reshape.232 = bf16[2,2,524288]{2,1,0:T(2,128)(2,1)} reshape(bf16[8192,16,16]{2,1,0:T(8,128)(2,1)} %bitcast.77) | data formatting | bytes 8388608
  373.6 12.0 %all_to_all.43 = bf16[2,2,524288]{2,1,0:T(2,128)(2,1)} all-to-all(bf16[2,2,524288]{2,1,0:T(2,128)(2,1)} %reshape.232), channel_id=1, replica_groups=mesh['ctx'=16,'head'=2] {'head'}, dimensions={0} | all-to-all | bytes 8388608 | tf_op jit(solution)/shard_map/all_to_all | solution.py:48
  385.7 40.9 %reshape.233 = bf16[8192,16,16]{2,1,0:T(8,128)(2,1)} reshape(bf16[2,2,524288]{2,1,0:T(2,128)(2,1)} %all_to_all.43) | data formatting | bytes 8388608
  426.6 24.1 %fusion.20 = (bf16[16,16,4096]{1,0,2:T(8,128)(2,1)}, bf16[16,16,4096]{1,0,2:T(8,128)(2,1)}) fusion(bf16[16,16,8192]{1,0,2:T(8,128)(2,1)} %bitcast.78), kind=kLoop, calls=%fused_computation.74 | loop fusion | bytes 8388608 | tf_op jit(solution)/shard_map/slice.6
  450.7 15.2 %copy.62 = bf16[16,16,4096]{2,1,0:T(8,128)(2,1)S(1)} copy(bf16[16,16,4096]{1,0,2:T(8,128)(2,1)} %get-tuple-element.184) | data formatting | bytes 4194304
  465.8 16.2 %copy.63 = bf16[16,16,4096]{2,1,0:T(8,128)(2,1)} copy(bf16[16,16,4096]{1,0,2:T(8,128)(2,1)} %get-tuple-element.185) | data formatting | bytes 4194304
  491.2 188.9 %while.15 = (s32[]{:T(128)}, f32[256,4,8]{0,2,1:T(8,128)S(1)}, f32[256,4,8]{0,2,1:T(8,128)S(1)}, f32[256,4,8,128]{0,3,2,1:T(8,128)}, s32[9]{0:T(128)S(1)}, /*ind...) while((s32[]{:T(128)}, f32[256,4,8]{0,2,1:T(8,128)S(1)}, ...), condition=%wide.region_8.11_spmd.clone, body=%wide.region_5.10_spmd.clone.sunk | while | flops 1104388608 | bytes 39064768 | solution.py:134
  523.1 9.1 %bitcast_add_fusion.2 = f32[256,4,8,128]{0,3,2,1:T(8,128)} fusion(f32[256,4,8,128]{0,3,2,1:T(8,128)} %get-tuple-element.296, f32[256,4,8]{0,2,1:T(8,128)S(1)} %get-tuple-element.277, pred[]{:T(512)S(6)} %compare.11, bf16[256,4,128,1]{0,2,3,1:T(8,128)(2,1)S(1)} %bitcast.88, f32[4,256,256,8]{2,1,3,0:T(8,128)} %get-tuple-element.275, ...), kind=kOutput, calls=%fused_computation.13.clone.1 | convolution fusion | flops 550502400 | bytes 17170432 | tf_op jit(solution)/shard_map/while/body/eval_jaxpr/tkgs,skd->tkgd/dot_general | solution.py:116
  544.3 9.1 %bitcast_add_fusion.2 = f32[256,4,8,128]{0,3,2,1:T(8,128)} fusion(f32[256,4,8,128]{0,3,2,1:T(8,128)} %get-tuple-element.296, f32[256,4,8]{0,2,1:T(8,128)S(1)} %get-tuple-element.277, pred[]{:T(512)S(6)} %compare.11, bf16[256,4,128,1]{0,2,3,1:T(8,128)(2,1)S(1)} %bitcast.88, f32[4,256,256,8]{2,1,3,0:T(8,128)} %get-tuple-element.275, ...), kind=kOutput, calls=%fused_computation.13.clone.1 | convolution fusion | flops 550502400 | bytes 17170432 | tf_op jit(solution)/shard_map/while/body/eval_jaxpr/tkgs,skd->tkgd/dot_general | solution.py:116
  565.4 9.1 %bitcast_add_fusion.2 = f32[256,4,8,128]{0,3,2,1:T(8,128)} fusion(f32[256,4,8,128]{0,3,2,1:T(8,128)} %get-tuple-element.296, f32[256,4,8]{0,2,1:T(8,128)S(1)} %get-tuple-element.277, pred[]{:T(512)S(6)} %compare.11, bf16[256,4,128,1]{0,2,3,1:T(8,128)(2,1)S(1)} %bitcast.88, f32[4,256,256,8]{2,1,3,0:T(8,128)} %get-tuple-element.275, ...), kind=kOutput, calls=%fused_computation.13.clone.1 | convolution fusion | flops 550502400 | bytes 17170432 | tf_op jit(solution)/shard_map/while/body/eval_jaxpr/tkgs,skd->tkgd/dot_general | solution.py:116
  586.5 9.1 %bitcast_add_fusion.2 = f32[256,4,8,128]{0,3,2,1:T(8,128)} fusion(f32[256,4,8,128]{0,3,2,1:T(8,128)} %get-tuple-element.296, f32[256,4,8]{0,2,1:T(8,128)S(1)} %get-tuple-element.277, pred[]{:T(512)S(6)} %compare.11, bf16[256,4,128,1]{0,2,3,1:T(8,128)(2,1)S(1)} %bitcast.88, f32[4,256,256,8]{2,1,3,0:T(8,128)} %get-tuple-element.275, ...), kind=kOutput, calls=%fused_computation.13.clone.1 | convolution fusion | flops 550502400 | bytes 17170432 | tf_op jit(solution)/shard_map/while/body/eval_jaxpr/tkgs,skd->tkgd/dot_general | solution.py:116
  607.6 9.1 %bitcast_add_fusion.2 = f32[256,4,8,128]{0,3,2,1:T(8,128)} fusion(f32[256,4,8,128]{0,3,2,1:T(8,128)} %get-tuple-element.296, f32[256,4,8]{0,2,1:T(8,128)S(1)} %get-tuple-element.277, pred[]{:T(512)S(6)} %compare.11, bf16[256,4,128,1]{0,2,3,1:T(8,128)(2,1)S(1)} %bitcast.88, f32[4,256,256,8]{2,1,3,0:T(8,128)} %get-tuple-element.275, ...), kind=kOutput, calls=%fused_computation.13.clone.1 | convolution fusion | flops 550502400 | bytes 17170432 | tf_op jit(solution)/shard_map/while/body/eval_jaxpr/tkgs,skd->tkgd/dot_general | solution.py:116
  628.7 9.1 %bitcast_add_fusion.2 = f32[256,4,8,128]{0,3,2,1:T(8,128)} fusion(f32[256,4,8,128]{0,3,2,1:T(8,128)} %get-tuple-element.296, f32[256,4,8]{0,2,1:T(8,128)S(1)} %get-tuple-element.277, pred[]{:T(512)S(6)} %compare.11, bf16[256,4,128,1]{0,2,3,1:T(8,128)(2,1)S(1)} %bitcast.88, f32[4,256,256,8]{2,1,3,0:T(8,128)} %get-tuple-element.275, ...), kind=kOutput, calls=%fused_computation.13.clone.1 | convolution fusion | flops 550502400 | bytes 17170432 | tf_op jit(solution)/shard_map/while/body/eval_jaxpr/tkgs,skd->tkgd/dot_general | solution.py:116
  649.9 9.1 %bitcast_add_fusion.2 = f32[256,4,8,128]{0,3,2,1:T(8,128)} fusion(f32[256,4,8,128]{0,3,2,1:T(8,128)} %get-tuple-element.296, f32[256,4,8]{0,2,1:T(8,128)S(1)} %get-tuple-element.277, pred[]{:T(512)S(6)} %compare.11, bf16[256,4,128,1]{0,2,3,1:T(8,128)(2,1)S(1)} %bitcast.88, f32[4,256,256,8]{2,1,3,0:T(8,128)} %get-tuple-element.275, ...), kind=kOutput, calls=%fused_computation.13.clone.1 | convolution fusion | flops 550502400 | bytes 17170432 | tf_op jit(solution)/shard_map/while/body/eval_jaxpr/tkgs,skd->tkgd/dot_general | solution.py:116
  671.0 9.1 %bitcast_add_fusion.2 = f32[256,4,8,128]{0,3,2,1:T(8,128)} fusion(f32[256,4,8,128]{0,3,2,1:T(8,128)} %get-tuple-element.296, f32[256,4,8]{0,2,1:T(8,128)S(1)} %get-tuple-element.277, pred[]{:T(512)S(6)} %compare.11, bf16[256,4,128,1]{0,2,3,1:T(8,128)(2,1)S(1)} %bitcast.88, f32[4,256,256,8]{2,1,3,0:T(8,128)} %get-tuple-element.275, ...), kind=kOutput, calls=%fused_computation.13.clone.1 | convolution fusion | flops 550502400 | bytes 17170432 | tf_op jit(solution)/shard_map/while/body/eval_jaxpr/tkgs,skd->tkgd/dot_general | solution.py:116
  (186 shorter events, 251.0 us)
Async XLA Ops:
  0.0 12.5 %copy-start = (bf16[128,8192]{1,0:T(8,128)(2,1)S(1)}, bf16[128,8192]{1,0:T(8,128)(2,1)}, u32[]{:S(2)}) copy-start(bf16[128,8192]{1,0:T(8,128)(2,1)} %param.11) | copy-start | bytes 6291460
  5.4 20.2 %all-to-all-start.2 = ((bf16[16,16,1024]{2,1,0:T(8,128)(2,1)}), bf16[16,16,1024]{2,1,0:T(8,128)(2,1)S(1)}, u32[]{:S(2)}, u32[]{:S(2)}) async-start(bf16[16,16,1024]{2,1,0:T(8,128)(2,1)} %get-tuple-element.193), calls=%async_computation.2 | async-start | bytes 1048576 | tf_op jit(solution)/shard_map/all_to_all | solution.py:63
  25.5 22.1 %all-to-all-start = ((bf16[16,16,1024]{2,1,0:T(8,128)(2,1)}), bf16[16,16,1024]{2,1,0:T(8,128)(2,1)S(1)}, u32[]{:S(2)}, u32[]{:S(2)}) async-start(bf16[16,16,1024]{2,1,0:T(8,128)(2,1)} %get-tuple-element.192), calls=%async_computation | async-start | bytes 1048576 | tf_op jit(solution)/shard_map/all_to_all | solution.py:56
  47.6 14.2 %all-to-all-start.3 = ((bf16[2,2,65536]{2,1,0:T(2,128)(2,1)}), bf16[2,2,65536]{2,1,0:T(2,128)(2,1)S(1)}, u32[]{:S(2)}, u32[]{:S(2)}) async-start(bf16[2,2,65536]{2,1,0:T(2,128)(2,1)} %reshape.228), calls=%async_computation.3 | async-start | bytes 1048576 | tf_op jit(solution)/shard_map/all_to_all | solution.py:62
  65.9 7.7 %copy-start.2 = (s32[256]{0:T(256)S(1)}, s32[256]{0:T(256)}, u32[]{:S(2)}) copy-start(s32[256]{0:T(256)} %param.15) | copy-start | bytes 3076
  65.9 251.0 %all-to-all-start.4 = ((bf16[16,16,8192]{2,1,0:T(8,128)(2,1)}), bf16[16,16,8192]{2,1,0:T(8,128)(2,1)}, u32[]{:S(2)}, u32[]{:S(2)}) async-start(bf16[16,16,8192]{2,1,0:T(8,128)(2,1)} %select_select_fusion), calls=%async_computation.4 | async-start | bytes 8388608 | tf_op jit(solution)/shard_map/all_to_all | solution.py:49
  100.2 13.9 %copy-start.3 = (s32[4]{0:T(128)S(1)}, s32[4]{0:T(128)}, u32[]{:S(2)}) copy-start(s32[4]{0:T(128)} %param.14) | copy-start | bytes 52
  103.2 120.2 %collective-permute-start = (bf16[2,256,512]{2,1,0:T(8,128)(2,1)S(1)}, bf16[2,256,512]{2,1,0:T(8,128)(2,1)}, u32[]{:S(2)}, u32[]{:S(2)}) collective-permute-start(bf16[2,256,512]{2,1,0:T(8,128)(2,1)S(1)} %pad_maximum_fusion.3), channel_id=1, source_target_pairs={{0,16},{2,18},{4,20},{6,22},{8,24},{10,26},{12,28},{14,30},{1,17},... | collective-permute-start | bytes 1572872 | tf_op jit(solution)/shard_map/ppermute | solution.py:13
  108.3 126.4 %collective-permute-start.1 = (bf16[2,256,512]{2,1,0:T(8,128)(2,1)S(1)}, bf16[2,256,512]{2,1,0:T(8,128)(2,1)S(1)}, u32[]{:S(2)}, u32[]{:S(2)}) collective-permute-start(bf16[2,256,512]{2,1,0:T(8,128)(2,1)S(1)} %pad_maximum_fusion.3), channel_id=1, source_target_pairs={{0,14},{2,16},{4,18},{6,20},{8,22},{10,24},{12,26},{14,28},{16,30}... | collective-permute-start | bytes 1572872 | tf_op jit(solution)/shard_map/ppermute | solution.py:13
  110.2 144.3 %collective-permute-start.2 = (bf16[2,256,512]{2,1,0:T(8,128)(2,1)S(1)}, bf16[2,256,512]{2,1,0:T(8,128)(2,1)S(1)}, u32[]{:S(2)}, u32[]{:S(2)}) collective-permute-start(bf16[2,256,512]{2,1,0:T(8,128)(2,1)S(1)} %pad_maximum_fusion.3), channel_id=1, source_target_pairs={{0,12},{2,14},{4,16},{6,18},{8,20},{10,22},{12,24},{14,26},{16,28}... | collective-permute-start | bytes 1572872 | tf_op jit(solution)/shard_map/ppermute | solution.py:13
  112.2 158.5 %collective-permute-start.3 = (bf16[2,256,512]{2,1,0:T(8,128)(2,1)S(1)}, bf16[2,256,512]{2,1,0:T(8,128)(2,1)S(1)}, u32[]{:S(2)}, u32[]{:S(2)}) collective-permute-start(bf16[2,256,512]{2,1,0:T(8,128)(2,1)S(1)} %pad_maximum_fusion.3), channel_id=1, source_target_pairs={{0,10},{2,12},{4,14},{6,16},{8,18},{10,20},{12,22},{14,24},{16,26}... | collective-permute-start | bytes 1572872 | tf_op jit(solution)/shard_map/ppermute | solution.py:13
  114.3 167.6 %collective-permute-start.4 = (bf16[2,256,512]{2,1,0:T(8,128)(2,1)S(1)}, bf16[2,256,512]{2,1,0:T(8,128)(2,1)S(1)}, u32[]{:S(2)}, u32[]{:S(2)}) collective-permute-start(bf16[2,256,512]{2,1,0:T(8,128)(2,1)S(1)} %pad_maximum_fusion.3), channel_id=1, source_target_pairs={{0,8},{2,10},{4,12},{6,14},{8,16},{10,18},{12,20},{14,22},{16,24},... | collective-permute-start | bytes 1572872 | tf_op jit(solution)/shard_map/ppermute | solution.py:13
  223.5 69.6 %collective-permute-start.5 = (bf16[2,256,512]{2,1,0:T(8,128)(2,1)S(1)}, bf16[2,256,512]{2,1,0:T(8,128)(2,1)S(1)}, u32[]{:S(2)}, u32[]{:S(2)}) collective-permute-start(bf16[2,256,512]{2,1,0:T(8,128)(2,1)S(1)} %pad_maximum_fusion.3), channel_id=1, source_target_pairs={{0,6},{2,8},{4,10},{6,12},{8,14},{10,16},{12,18},{14,20},{16,22},{... | collective-permute-start | bytes 1572872 | tf_op jit(solution)/shard_map/ppermute | solution.py:13
  234.7 69.6 %collective-permute-start.6 = (bf16[2,256,512]{2,1,0:T(8,128)(2,1)S(1)}, bf16[2,256,512]{2,1,0:T(8,128)(2,1)S(1)}, u32[]{:S(2)}, u32[]{:S(2)}) collective-permute-start(bf16[2,256,512]{2,1,0:T(8,128)(2,1)S(1)} %pad_maximum_fusion.3), channel_id=1, source_target_pairs={{0,4},{2,6},{4,8},{6,10},{8,12},{10,14},{12,16},{14,18},{16,20},{1... | collective-permute-start | bytes 1572872 | tf_op jit(solution)/shard_map/ppermute | solution.py:13
  254.6 59.9 %collective-permute-start.7 = (bf16[2,256,512]{2,1,0:T(8,128)(2,1)S(1)}, bf16[2,256,512]{2,1,0:T(8,128)(2,1)S(1)}, u32[]{:S(2)}, u32[]{:S(2)}) collective-permute-start(bf16[2,256,512]{2,1,0:T(8,128)(2,1)S(1)} %pad_maximum_fusion.3), channel_id=1, source_target_pairs={{0,2},{2,4},{4,6},{6,8},{8,10},{10,12},{12,14},{14,16},{16,18},{18... | collective-permute-start | bytes 1572872 | tf_op jit(solution)/shard_map/ppermute | solution.py:13
  680.1 8.3 %copy-start.1 = (bf16[128,8192]{1,0:T(8,128)(2,1)S(1)}, bf16[128,8192]{1,0:T(8,128)(2,1)}, u32[]{:S(2)}) copy-start(bf16[128,8192]{1,0:T(8,128)(2,1)} %param.11) | copy-start | bytes 6291460
where the time goes:
time: 700 us; the launch traced here: 689 us
  local copies, waits for them, and re-layouts  236 us (34%)
  waiting for transfers between devices  201 us (29%)
  matrix products  123 us (18%)
  other arithmetic  61.9 us (9%)
  starting transfers between devices  42.9 us (6%)
  blocking collectives  16.2 us (2%)
    ppermute x8, waiting for transfers between devices, shifted(): return lax.ppermute(block, axis, route)  191 us
    unnamed x30, local copies, waits for them, and re-layouts  133 us
    dot_general x9, matrix products, absorb(): jnp.einsum('tkgs,skd->tkgd', weights.astype(jnp.bfloat16), values_split,...  80.9 us
    dot_general x9, matrix products, absorb(): jnp.einsum('tkgd,skd->tkgs', queries, keys_split, preferred_element_type=...  42.4 us
    reduce_sum x9, other arithmetic, absorb(): running_sum = running_sum * factor + jnp.sum(weights, axis=-1)  40.6 us
    another operation x2, local copies, waits for them, and re-layouts  28.4 us
    all_to_all x1, local copies, waits for them, and re-layouts, body(): lax.all_to_all(sending[0], 'ctx', split_axis=0, concat_axis=0, tiled=True)  27.6 us
    ppermute x8, starting transfers between devices, shifted(): return lax.ppermute(block, axis, route)  18.6 us
  transfers between devices with their start and end apart: 12, of which 9 were waited for; matrix products, arithmetic and copies ran while one was open for 9% of the time, Pallas kernels for 0%

commit v1 on v0

v1 whole, which is shorter than its diff:
```python
import functools

import jax
import jax.numpy as jnp
import numpy as np
from jax import lax
from jax.experimental import pallas as pl
from jax.experimental.pallas import tpu as pltpu
from jax.sharding import PartitionSpec as P

HD = 128
SPAN = 8
MASKED = -1e30
EXP2_SCALE = float(HD ** (-0.5) * np.log2(np.e))
VMEM_LIMIT = 48 * 1024 * 1024
ANY = pl.BlockSpec(memory_space=pl.ANY)


def pack_kernel(chunks, place_ref, loader_ref, query, key, value, *refs):
    outs, (own, other, sems) = refs[:chunks], refs[chunks:]
    per_loader = query.shape[0]
    group = loader_ref[1]
    half = key.shape[1] // 2
    width = outs[0].shape[2]
    copies = []

    def start(src, dst):
        copy = pltpu.make_async_copy(src, dst, sems.at[len(copies)])
        copy.start()
        copies.append(copy)

    for out, which in ((own, group), (other, 1 - group)):
        columns = pl.ds(pl.multiple_of(which * half, half), half)
        start(key.at[:, columns], out.at[:, pl.ds(0, half)])
        start(value.at[:, columns], out.at[:, pl.ds(half, half)])
    for chunk in range(chunks):
        for j in range(per_loader):
            target = place_ref[loader_ref[0] * per_loader + j] // loader_ref[2]
            for side in range(2):
                start(
                    query.at[j, :, pl.ds((side * chunks + chunk) * width, width)],
                    outs[chunk].at[target * 2 + side],
                )
    for copy in copies:
        copy.wait()


def pack(query, key, value, block_place, loader, shard_blocks, slots, chunks):
    rows, columns = query.shape
    per_loader = block_place.shape[0] // slots
    block_rows = rows // per_loader
    width = columns // 2 // chunks
    half = key.shape[1] // 2
    blocks = query.reshape(per_loader, block_rows, columns)
    if block_rows % 16:
        group = loader % 2
        assigned = lax.dynamic_slice_in_dim(block_place, loader * per_loader, per_loader)
        targets = assigned // shard_blocks
        matched = targets[None, :] == jnp.arange(slots // 2, dtype=jnp.int32)[:, None]
        sources = jnp.argmax(matched, axis=1)
        picked = jnp.take(blocks, sources, axis=0)
        picked = picked.reshape(slots // 2, block_rows, 2, chunks, width)
        sends = [
            jnp.swapaxes(picked[:, :, :, chunk], 1, 2).reshape(slots, block_rows, width)
            for chunk in range(chunks)
        ]
        pairs = [
            jnp.concatenate(
                [lax.dynamic_slice_in_dim(x, which * half, half, 1) for x in (key, value)], axis=1
            )
            for which in (group, 1 - group)
        ]
        return sends, pairs[0], pairs[1]
    scalars = jnp.stack([loader, loader % 2, jnp.int32(shard_blocks)]).astype(jnp.int32)
    outs = pl.pallas_call(
        functools.partial(pack_kernel, chunks),
        out_shape=[jax.ShapeDtypeStruct((slots, block_rows, width), query.dtype)] * chunks
        + [jax.ShapeDtypeStruct((rows, 2 * half), key.dtype)] * 2,
        grid_spec=pltpu.PrefetchScalarGridSpec(
            num_scalar_prefetch=2,
            grid=(1,),
            in_specs=[ANY] * 3,
            out_specs=[ANY] * (chunks + 2),
            scratch_shapes=[pltpu.SemaphoreType.DMA((4 + 2 * chunks * per_loader,))],
        ),
        name="pack",
    )(block_place, scalars, blocks, key, value)
    return outs[:chunks], outs[chunks], outs[chunks + 1]


def window_kernel(count, rows_ref, same, cross, out, sem):
    limit = same.shape[0]

    def start(w, carry):
        source = rows_ref[w]

        @pl.when(source < limit)
        def _():
            pltpu.make_async_copy(same.at[source], out.at[w], sem).start()

        @pl.when(source >= limit)
        def _():
            pltpu.make_async_copy(cross.at[source - limit], out.at[w], sem).start()

        return carry

    lax.fori_loop(0, count, start, 0)
    pltpu.make_async_copy(out, out, sem).wait()


def pick_window(sources, same, cross):
    count = sources.shape[0]
    if same.shape[1] % 16:
        return jnp.take(jnp.concatenate([same, cross]), sources, axis=0)
    return pl.pallas_call(
        functools.partial(window_kernel, count),
        out_shape=jax.ShapeDtypeStruct((count,) + same.shape[1:], same.dtype),
        grid_spec=pltpu.PrefetchScalarGridSpec(
            num_scalar_prefetch=1,
            grid=(1,),
            in_specs=[ANY, ANY],
            out_specs=ANY,
            scratch_shapes=[pltpu.SemaphoreType.DMA(())],
        ),
        name="window",
        cost_estimate=pl.CostEstimate(
            flops=0, transcendentals=0, bytes_accessed=4 * count * same.shape[1] * same.shape[2]
        ),
    )(sources, same, cross)


def attend_kernel(
    docs, heads, tile, slot_ref, lengths_ref, shard_ref, *refs
):
    arrived, keys, values = refs[0], refs[1], refs[2]
    out, queries, maxes, sums, sem = refs[-5:]
    blocks, block_rows, width = queries.shape
    rows = blocks * block_rows
    copies = []
    for i in range(blocks):
        copy = pltpu.make_async_copy(arrived.at[slot_ref[i]], queries.at[i], sem.at[i])
        copy.start()
        copies.append(copy)
    first_row = shard_ref[0] * rows
    query_rows = first_row + lax.broadcasted_iota(jnp.int32, (1, rows), 1)
    starts = jnp.zeros((1, rows), jnp.int32)
    first_start = jnp.int32(0)
    end = jnp.int32(0)
    for d in range(docs):
        length = lengths_ref[d]
        end = end + length
        starts = starts + jnp.where(query_rows >= end, length, 0)
        first_start = first_start + jnp.where(first_row >= end, length, 0)
    tiles = keys.shape[0] // tile
    window_start = first_row + rows - keys.shape[0]
    diagonal = tiles - 1
    first_tile = (first_start - window_start) // tile
    for h in range(heads):
        maxes[h] = jnp.full((1, rows), MASKED, jnp.float32)
        sums[h] = jnp.zeros(sums.shape[1:], jnp.float32)
    for copy in copies:
        copy.wait()

    def step(index, masked, last):
        span = pl.ds(pl.multiple_of(index * tile, tile), tile)
        tile_keys = keys[span, :]
        tile_values = values[span, :]
        extended = jnp.concatenate([tile_values, jnp.ones((tile, HD), tile_values.dtype)], axis=1)
        turned = extended.T[: HD + 16]
        if masked:
            key_rows = window_start + index * tile + lax.broadcasted_iota(jnp.int32, (tile, rows), 0)
            visible = (key_rows >= starts) & (key_rows <= query_rows)
        if last:
            later = starts >= first_row

        def score(h):
            query = queries[:, :, h * HD : (h + 1) * HD].reshape(rows, HD)
            return lax.dot_general(
                tile_keys, query, (((1,), (1,)), ((), ())), preferred_element_type=jnp.float32
            )

        ahead = score(0)
        for h in range(heads):
            scores = ahead
            if h + 1 < heads:
                ahead = score(h + 1)
            if masked:
                scores = jnp.where(visible, scores, MASKED)
            old = maxes[h]
            if last:
                old = jnp.where(later, MASKED, old)
            new = jnp.maximum(old, jnp.max(scores, axis=0, keepdims=True))
            scaled = new * EXP2_SCALE
            weights = jnp.exp2(scores * EXP2_SCALE - scaled).astype(jnp.bfloat16)
            factor = jnp.exp2(old * EXP2_SCALE - scaled)
            product = jnp.dot(turned, weights, preferred_element_type=jnp.float32)
            total = sums[h] * factor + product
            if last:
                result = total[:HD] / total[HD : HD + 1]
                out[:, h * HD : (h + 1) * HD] = result.T.astype(out.dtype)
            else:
                maxes[h] = new
                sums[h] = total

    @pl.when(first_tile < diagonal)
    def _():
        step(first_tile, True, False)

    def middle(index, carry):
        step(index, False, False)
        return carry

    lax.fori_loop(first_tile + 1, diagonal, middle, 0)
    step(diagonal, True, True)


def attend(arrived, window, slots, doc_lengths, shard, chunk, chunks, result, shard_rows):
    block_rows, width = arrived.shape[1:]
    blocks = shard_rows // block_rows
    if block_rows % 16:
        arrived = jnp.take(arrived, slots, axis=0).reshape(shard_rows // 16, 16, width)
        block_rows, blocks = 16, shard_rows // 16
        slots = jnp.arange(blocks, dtype=jnp.int32)
    heads = width // HD
    key_heads = window.shape[1] // 2 // HD
    per_key = window.shape[0]
    aliased = [] if result is None else [result]
    return pl.pallas_call(
        functools.partial(attend_kernel, doc_lengths.shape[0], heads, shard_rows),
        out_shape=jax.ShapeDtypeStruct((shard_rows, chunks * width), arrived.dtype),
        grid_spec=pltpu.PrefetchScalarGridSpec(
            num_scalar_prefetch=3,
            grid=(1,),
            in_specs=[
                ANY,
                pl.BlockSpec((per_key, HD), lambda i, *_: (0, chunk)),
                pl.BlockSpec((per_key, HD), lambda i, *_: (0, key_heads + chunk)),
            ]
            + [ANY] * len(aliased),
            out_specs=pl.BlockSpec((shard_rows, width), lambda i, *_: (0, chunk)),
            scratch_shapes=[
                pltpu.VMEM((blocks, block_rows, width), arrived.dtype),
                pltpu.VMEM((heads, 1, shard_rows), jnp.float32),
                pltpu.VMEM((heads, HD + 16, shard_rows), jnp.float32),
                pltpu.SemaphoreType.DMA((blocks,)),
            ],
        ),
        input_output_aliases={6: 0} if aliased else {},
        compiler_params=pltpu.CompilerParams(vmem_limit_bytes=VMEM_LIMIT),
        name=f"attend{chunk}",
        cost_estimate=pl.CostEstimate(
            flops=4 * shard_rows * per_key * width,
            transcendentals=shard_rows * per_key * heads,
            bytes_accessed=4 * shard_rows * width + 4 * per_key * HD,
        ),
    )(slots, doc_lengths, shard, arrived, window, window, *aliased)


def body(query, key, value, doc_lengths, block_place):
    ctx_count = lax.axis_size("ctx")
    head_count = lax.axis_size("head")
    loaded_rows = query.shape[0]
    shard_rows = loaded_rows * head_count
    block_rows = shard_rows // ctx_count
    per_loader = loaded_rows // block_rows
    shard_blocks = shard_rows // block_rows
    shard = lax.axis_index("ctx").astype(jnp.int32)
    group = lax.axis_index("head").astype(jnp.int32)
    loader = shard * head_count + group
    slots = ctx_count * head_count
    chunks = key.shape[1] // head_count // HD
    sends, own, other = pack(
        query, key, value, block_place, loader, shard_blocks, slots, chunks
    )
    swapped = lax.ppermute(other, "head", [(0, 1), (1, 0)])
    same = lax.all_gather(own, "ctx", tiled=True)
    cross = lax.all_gather(swapped, "ctx", tiled=True)
    arrived = [
        lax.all_to_all(send, ("ctx", "head"), split_axis=0, concat_axis=0, tiled=True)
        for send in sends
    ]
    wanted = (shard - SPAN) * shard_blocks + jnp.arange((SPAN + 1) * shard_blocks, dtype=jnp.int32)
    wanted = jnp.maximum(wanted, 0)
    places = jnp.arange(block_place.shape[0], dtype=jnp.int32)
    inverse = jnp.sum(jnp.where(wanted[:, None] == block_place[None, :], places[None, :], 0), axis=1)
    source = inverse // per_loader
    half_blocks = ctx_count * per_loader
    sources = (
        source // head_count * per_loader
        + inverse % per_loader
        + jnp.where(source % head_count == group, 0, half_blocks)
    )
    width = same.shape[1]
    window = pick_window(
        sources,
        same.reshape(half_blocks, block_rows, width),
        cross.reshape(half_blocks, block_rows, width),
    )
    window = window.reshape((SPAN + 1) * shard_rows, width)
    result = None
    for chunk in range(chunks):
        result = attend(
            arrived[chunk],
            window,
            source[SPAN * shard_blocks :],
            doc_lengths,
            shard[None],
            chunk,
            chunks,
            result,
            shard_rows,
        )
    return result


def solution(mesh):
    placed = (
        P(("ctx", "head"), None),
        P(("ctx", "head"), None),
        P(("ctx", "head"), None),
        P(),
        P(),
    )
    return jax.shard_map(
        body, mesh=mesh, in_specs=placed, out_specs=P("ctx", "head"), check_vma=False
    )
```

time: 700 us -> 492 us (0.70); the launches traced: 689 us -> 492 us
  Pallas kernels: 0 us -> 278 us
  local copies, waits for them, and re-layouts: 236 us -> 6.62 us
  waiting for transfers between devices: 201 us -> 56.2 us
  matrix products: 123 us -> 0 us
  blocking collectives: 16.2 us -> 130 us
  other arithmetic: 61.9 us -> 1.46 us
  starting transfers between devices: 42.9 us -> 5.86 us
  between operations: 0.79 us -> 13.6 us
    pallas_call x0 -> x6, Pallas kernels: none -> 278 us  [the longest x1 145 us: pick_window(): pl.pallas_call(functools.partial(window_kernel, count), out_shape=jax.Sha...]
    ppermute x8 -> x1, waiting for transfers between devices: 191 us -> 1.73 us  [body(): swapped = lax.ppermute(other, 'head', [(0, 1), (1, 0)])]
    unnamed x30 -> x16, local copies, waits for them, and re-layouts: 133 us -> 6.62 us
    dot_general x18 -> x0, matrix products: 123 us -> none  [the longest x9 80.9 us: absorb(): jnp.einsum('tkgs,skd->tkgd', weights.astype(jnp.bfloat16), values_split,...]
    all_to_all x2 -> x3, blocking collectives: 16.2 us -> 130 us  [body(): lax.all_to_all(send, ('ctx', 'head'), split_axis=0, concat_axis=0, tiled=...]
    all_gather x0 -> x2, waiting for transfers between devices: none -> 54.4 us  [the longest x1 54.4 us: body(): cross = lax.all_gather(swapped, 'ctx', tiled=True)]
    reduce_sum x11 -> x1, other arithmetic: 40.7 us -> 0.19 us  [body(): jnp.sum(jnp.where(wanted[:, None] == block_place[None, :], places[None, :...]
    all_to_all x3 -> x0, local copies, waits for them, and re-layouts: 37.1 us -> none  [the longest x1 27.6 us: body(): lax.all_to_all(sending[0], 'ctx', split_axis=0, concat_axis=0, tiled=True)]
  transfers between devices with their start and end apart: 12 -> 4, of which waited for: 9 -> 2; matrix products, arithmetic and copies ran while one was open for 9% -> 0% of each run, Pallas kernels for 0% -> 37%
where the time goes in v1:
time: 492 us
  Pallas kernels  278 us (57%)
  blocking collectives  130 us (26%)
  waiting for transfers between devices  56.2 us (11%)
  between operations  13.6 us (3%)
  local copies, waits for them, and re-layouts  6.62 us (1%)
  starting transfers between devices  5.86 us (1%)
    pallas_call x1, Pallas kernels, pick_window(): pl.pallas_call(functools.partial(window_kernel, count), out_shape=jax.Sha...  145 us
    all_to_all x3, blocking collectives, body(): lax.all_to_all(send, ('ctx', 'head'), split_axis=0, concat_axis=0, tiled=...  130 us
    pallas_call x1, Pallas kernels, pack(): pl.pallas_call(functools.partial(pack_kernel, chunks), out_shape=[jax.Sha...  81.8 us
    all_gather x1, waiting for transfers between devices, body(): cross = lax.all_gather(swapped, 'ctx', tiled=True)  54.4 us
    pallas_call x4, Pallas kernels, attend(): pl.pallas_call(functools.partial(attend_kernel, doc_lengths.shape[0], hea...  51.1 us
  transfers between devices with their start and end apart: 4, of which 2 were waited for; matrix products, arithmetic and copies ran while one was open for 0% of the time, Pallas kernels for 37%

profile of v1, /device:TPU:14, one launch (start us, length us, event | category | flops | bytes accessed | tf_op | source)
XLA Modules:
  0.0 491.8 jit_solution(5504684978620549270)
XLA Ops:
  6.5 0.7 pad_add_fusion.loader_ref
  7.2 81.8 %pack.1 = (bf16[32,16,1024]{2,1,0:T(8,128)(2,1)}, bf16[32,16,1024]{2,1,0:T(8,128)(2,1)}, bf16[32,16,1024]{2,1,0:T(8,128)(2,1)}, bf16[32,16,1024]{2,1,0:T(8,128)(...) custom-call(s32[256]{0:T(256)} %place_ref.1, s32[3]{0:T(128)} %pad_add_fusion.loader_ref, ...), custom_call_target="tpu_custom_call" | custom-call | tf_op jit(solution)/shard_map/pack/pallas_call | solution.py:75
  89.0 0.0 all-gather.3.cloned.1.call-update
  89.1 0.0 all-gather.5.cloned.1.call-start
  89.1 0.1 collective-permute-start
  89.2 1.7 collective-permute-done
  90.9 0.7 copy-done.6
  91.6 0.0 all-gather.5.cloned.1.call-update
  91.7 0.0 copy-start.4
  91.7 42.4 %all_to_all.20.refs_0_ = bf16[32,16,1024]{2,1,0:T(8,128)(2,1)S(1)} all-to-all(bf16[32,16,1024]{2,1,0:T(8,128)(2,1)} %get-tuple-element.14), channel_id=1, replica_groups=mesh['ctx'=16,'head'=2] {'ctx','head'}, dimensions={0} | all-to-all | bytes 2097152 | tf_op jit(solution)/shard_map/all_to_all | solution.py:279
  134.0 51.6 %all_to_all.21.refs_0_ = bf16[32,16,1024]{2,1,0:T(8,128)(2,1)S(1)} all-to-all(bf16[32,16,1024]{2,1,0:T(8,128)(2,1)S(1)} %copy-done.5), channel_id=1, replica_groups=mesh['ctx'=16,'head'=2] {'ctx','head'}, dimensions={0} | all-to-all | bytes 2097152 | tf_op jit(solution)/shard_map/all_to_all | solution.py:279
  185.7 36.4 %all_to_all.22.refs_0_ = bf16[32,16,1024]{2,1,0:T(8,128)(2,1)} all-to-all(bf16[32,16,1024]{2,1,0:T(8,128)(2,1)S(1)} %copy-done.4), channel_id=1, replica_groups=mesh['ctx'=16,'head'=2] {'ctx','head'}, dimensions={0} | all-to-all | bytes 2097152 | tf_op jit(solution)/shard_map/all_to_all | solution.py:279
  222.0 5.7 %all-to-all-start = ((bf16[32,16,1024]{2,1,0:T(8,128)(2,1)}), bf16[32,16,1024]{2,1,0:T(8,128)(2,1)S(1)}, u32[]{:S(2)}, u32[]{:S(2)}) async-start(bf16[32,16,1024]{2,1,0:T(8,128)(2,1)} %get-tuple-element.11), calls=%async_computation | async-start | bytes 2097152 | tf_op jit(solution)/shard_map/all_to_all | solution.py:279
  227.8 0.2 select_reduce_fusion
  228.0 0.6 fusion.1
  228.6 54.4 %all-gather.5.cloned.1.call-done = bf16[2048,1024]{1,0:T(8,128)(2,1)} async-done(((bf16[128,1024]{1,0:T(8,128)(2,1)}), bf16[2048,1024]{1,0:T(8,128)(2,1)}) %all-gather.5.cloned.1.call-update) | async-done | bytes 4194320 | tf_op jit(solution)/shard_map/all_gather | solution.py:277
  283.0 144.9 %window.1 = bf16[144,16,1024]{2,1,0:T(8,128)(2,1)} custom-call(s32[144]{0:T(256)} %get-tuple-element.17.rows_ref, bf16[128,16,1024]{2,1,0:T(8,128)(2,1)} %bitcast.15, bf16[128,16,1024]{2,1,0:T(8,128)(2,1)} %bitcast.16), custom_call_target="tpu_custom_call" | custom-call | bytes 9437184 | tf_op jit(solution)/shard_map/window/pallas_call | solution.py:115
  427.9 2.3 copy-done
  430.3 1.2 copy-done.2
  431.5 12.7 %attend0.1.refs_3_ = bf16[256,4096]{1,0:T(8,128)(2,1)} custom-call(s32[16]{0:T(128)S(1)} %slice.2.slot_ref, s32[4]{0:T(128)S(1)} %copy-done.3, s32[1]{0:T(128)} %bitcast.shard_ref, bf16[32,16,1024]{2,1,0:T(8,128)(2,1)S(1)} %copy-done.2, bf16[2304,1024]{1,0:T(8,128)(2,1)S(1)} %bitcast.7, bf16[2304,1024]{1,0:T(8,128)(2,1)S(1)} %bitcast.8), custom_call_target="tpu_custom_call" | custom-call | flops 2415919104 | bytes 2228224 | tf_op jit(solution)/shard_map/attend0/pallas_call | solution.py:228
  444.2 12.7 %attend1.1.refs_3_ = bf16[256,4096]{1,0:T(8,128)(2,1)} custom-call(s32[16]{0:T(128)S(1)} %slice.2.slot_ref, s32[4]{0:T(128)S(1)} %copy-done.3, s32[1]{0:T(128)} %bitcast.shard_ref, bf16[32,16,1024]{2,1,0:T(8,128)(2,1)S(1)} %all_to_all.21.refs_0_, bf16[2304,1024]{1,0:T(8,128)(2,1)S(1)} %bitcast.9, ...), custom_call_target="tpu_custom_call", output_to_operand_aliasing={{}: (6, {})} | custom-call | flops 2415919104 | bytes 2228224 | tf_op jit(solution)/shard_map/attend1/pallas_call | solution.py:228
  456.9 12.9 %attend2.1.refs_3_ = bf16[256,4096]{1,0:T(8,128)(2,1)} custom-call(s32[16]{0:T(128)S(1)} %slice.2.slot_ref, s32[4]{0:T(128)S(1)} %copy-done.3, s32[1]{0:T(128)} %bitcast.shard_ref, bf16[32,16,1024]{2,1,0:T(8,128)(2,1)S(1)} %all_to_all.20.refs_0_, bf16[2304,1024]{1,0:T(8,128)(2,1)S(1)} %bitcast.11, ...), custom_call_target="tpu_custom_call", output_to_operand_aliasing={{}: (6, {})} | custom-call | flops 2415919104 | bytes 2228224 | tf_op jit(solution)/shard_map/attend2/pallas_call | solution.py:228
  469.9 2.3 copy-done.1
  472.2 12.7 %attend3.1 = bf16[256,4096]{1,0:T(8,128)(2,1)} custom-call(s32[16]{0:T(128)S(1)} %slice.2.slot_ref, s32[4]{0:T(128)S(1)} %copy-done.3, s32[1]{0:T(128)} %bitcast.shard_ref, bf16[32,16,1024]{2,1,0:T(8,128)(2,1)S(1)} %all-to-all-done.refs_0_, bf16[2304,1024]{1,0:T(8,128)(2,1)S(1)} %bitcast.13, ...), custom_call_target="tpu_custom_call", output_to_operand_aliasing={{}: (6, {})} | custom-call | flops 2415919104 | bytes 2228224 | tf_op jit(solution)/shard_map/attend3/pallas_call | solution.py:228
  (16 shorter events, 0.0 us)
Async XLA Ops:
  6.5 222.1 %all-gather.3.cloned.1.call-start = ((), (), s32[]{:S(2)}) async-start(), calls=%async_computation.4 | async-start | bytes 4456448 | tf_op jit(solution)/shard_map/all_gather | solution.py:276
  89.0 45.0 %copy-start.5 = (bf16[32,16,1024]{2,1,0:T(8,128)(2,1)S(1)}, bf16[32,16,1024]{2,1,0:T(8,128)(2,1)}, u32[]{:S(2)}) copy-start(bf16[32,16,1024]{2,1,0:T(8,128)(2,1)} %get-tuple-element.15) | copy-start | bytes 3145732
  89.1 194.0 %all-gather.5.cloned.1.call-start = ((), (), s32[]{:S(2)}) async-start(), calls=%async_computation.5 | async-start | bytes 4456448 | tf_op jit(solution)/shard_map/all_gather | solution.py:277
  89.1 1.8 collective-permute-start
  90.9 0.7 copy-start.6
  91.7 94.0 %copy-start.4 = (bf16[32,16,1024]{2,1,0:T(8,128)(2,1)S(1)}, bf16[32,16,1024]{2,1,0:T(8,128)(2,1)}, u32[]{:S(2)}) copy-start(bf16[32,16,1024]{2,1,0:T(8,128)(2,1)} %get-tuple-element.16) | copy-start | bytes 3145732
  185.7 42.1 %copy-start.7 = (s32[256]{0:T(256)S(1)}, s32[256]{0:T(256)}, u32[]{:S(2)}) copy-start(s32[256]{0:T(256)} %place_ref.1) | copy-start | bytes 3076
  222.0 247.8 %all-to-all-start = ((bf16[32,16,1024]{2,1,0:T(8,128)(2,1)}), bf16[32,16,1024]{2,1,0:T(8,128)(2,1)S(1)}, u32[]{:S(2)}, u32[]{:S(2)}) async-start(bf16[32,16,1024]{2,1,0:T(8,128)(2,1)} %get-tuple-element.11), calls=%async_computation | async-start | bytes 2097152 | tf_op jit(solution)/shard_map/all_to_all | solution.py:279
  283.0 144.9 %copy-start.3 = (s32[4]{0:T(128)S(1)}, s32[4]{0:T(128)}, u32[]{:S(2)}) copy-start(s32[4]{0:T(128)} %lengths_ref.7) | copy-start | bytes 52
  427.9 2.3 copy-start
  430.3 1.2 copy-start.2
  469.9 2.3 copy-start.1
Sparse Core Ops, SparseCore 0:
  89.2 98.7 all-gather.2
  190.8 92.2 all-gather.4

commit v2 on v1

--- a/solution.py
+++ b/solution.py
@@ -79,54 +79,50 @@
         grid_spec=pltpu.PrefetchScalarGridSpec(
             num_scalar_prefetch=2,
             grid=(1,),
-            in_specs=[ANY] * 3,
+            in_specs=[
+                pl.BlockSpec(blocks.shape, lambda i, *_: (0, 0, 0)),
+                pl.BlockSpec(key.shape, lambda i, *_: (0, 0)),
+                pl.BlockSpec(value.shape, lambda i, *_: (0, 0)),
+            ],
             out_specs=[ANY] * (chunks + 2),
             scratch_shapes=[pltpu.SemaphoreType.DMA((4 + 2 * chunks * per_loader,))],
         ),
+        compiler_params=pltpu.CompilerParams(vmem_limit_bytes=VMEM_LIMIT),
         name="pack",
     )(block_place, scalars, blocks, key, value)
     return outs[:chunks], outs[chunks], outs[chunks + 1]
 
 
-def window_kernel(count, rows_ref, same, cross, out, sem):
-    limit = same.shape[0]
-
+def window_kernel(count, rows_ref, blocks, out, sem):
     def start(w, carry):
-        source = rows_ref[w]
-
-        @pl.when(source < limit)
-        def _():
-            pltpu.make_async_copy(same.at[source], out.at[w], sem).start()
-
-        @pl.when(source >= limit)
-        def _():
-            pltpu.make_async_copy(cross.at[source - limit], out.at[w], sem).start()
-
+        pltpu.make_async_copy(blocks.at[rows_ref[w]], out.at[w], sem).start()
         return carry
 
-    lax.fori_loop(0, count, start, 0)
+    lax.fori_loop(0, count, start, 0, unroll=8)
     pltpu.make_async_copy(out, out, sem).wait()
 
 
-def pick_window(sources, same, cross):
+def pick_window(sources, blocks):
     count = sources.shape[0]
-    if same.shape[1] % 16:
-        return jnp.take(jnp.concatenate([same, cross]), sources, axis=0)
+    shape = (count,) + blocks.shape[1:]
+    if blocks.shape[1] % 16:
+        return jnp.take(blocks, sources, axis=0)
     return pl.pallas_call(
         functools.partial(window_kernel, count),
-        out_shape=jax.ShapeDtypeStruct((count,) + same.shape[1:], same.dtype),
+        out_shape=jax.ShapeDtypeStruct(shape, blocks.dtype),
         grid_spec=pltpu.PrefetchScalarGridSpec(
             num_scalar_prefetch=1,
             grid=(1,),
-            in_specs=[ANY, ANY],
-            out_specs=ANY,
+            in_specs=[ANY],
+            out_specs=pl.BlockSpec(shape, lambda i, *_: (0, 0, 0)),
             scratch_shapes=[pltpu.SemaphoreType.DMA(())],
         ),
+        compiler_params=pltpu.CompilerParams(vmem_limit_bytes=VMEM_LIMIT),
         name="window",
         cost_estimate=pl.CostEstimate(
-            flops=0, transcendentals=0, bytes_accessed=4 * count * same.shape[1] * same.shape[2]
-        ),
-    )(sources, same, cross)
+            flops=0, transcendentals=0, bytes_accessed=4 * count * shape[1] * shape[2]
+        ),
+    )(sources, blocks)
 
 
 def attend_kernel(
@@ -273,8 +269,7 @@
         query, key, value, block_place, loader, shard_blocks, slots, chunks
     )
     swapped = lax.ppermute(other, "head", [(0, 1), (1, 0)])
-    same = lax.all_gather(own, "ctx", tiled=True)
-    cross = lax.all_gather(swapped, "ctx", tiled=True)
+    gathered = lax.all_gather(jnp.concatenate([own, swapped]), "ctx", tiled=True)
     arrived = [
         lax.all_to_all(send, ("ctx", "head"), split_axis=0, concat_axis=0, tiled=True)
         for send in sends
@@ -284,18 +279,13 @@
     places = jnp.arange(block_place.shape[0], dtype=jnp.int32)
     inverse = jnp.sum(jnp.where(wanted[:, None] == block_place[None, :], places[None, :], 0), axis=1)
     source = inverse // per_loader
-    half_blocks = ctx_count * per_loader
     sources = (
-        source // head_count * per_loader
+        source // head_count * (head_count * per_loader)
         + inverse % per_loader
-        + jnp.where(source % head_count == group, 0, half_blocks)
+        + jnp.where(source % head_count == group, 0, per_loader)
     )
-    width = same.shape[1]
-    window = pick_window(
-        sources,
-        same.reshape(half_blocks, block_rows, width),
-        cross.reshape(half_blocks, block_rows, width),
-    )
+    width = gathered.shape[1]
+    window = pick_window(sources, gathered.reshape(-1, block_rows, width))
     window = window.reshape((SPAN + 1) * shard_rows, width)
     result = None
     for chunk in range(chunks):

time: 492 us -> 267 us (0.54)
  the two profiles are of different devices: /device:TPU:14 before, /device:TPU:16 now
where the time goes in v2:
time: 267 us; the launch traced here: 264 us
  blocking collectives  147 us (55%)
  Pallas kernels  58.8 us (22%)
  waiting for transfers between devices  30.4 us (11%)
  between operations  13.6 us (5%)
  local copies, waits for them, and re-layouts  6.96 us (3%)
  starting transfers between devices  6.33 us (2%)
    all_to_all x3, blocking collectives, body(): lax.all_to_all(send, ('ctx', 'head'), split_axis=0, concat_axis=0, tiled=...  147 us
    pallas_call x4, Pallas kernels, attend(): pl.pallas_call(functools.partial(attend_kernel, doc_lengths.shape[0], hea...  51.1 us
    all_gather x1, waiting for transfers between devices, body(): lax.all_gather(jnp.concatenate([own, swapped]), 'ctx', tiled=True)  28.9 us
    unnamed x22, local copies, waits for them, and re-layouts  6.95 us
    all_to_all x1, starting transfers between devices, body(): lax.all_to_all(send, ('ctx', 'head'), split_axis=0, concat_axis=0, tiled=...  6.32 us
  transfers between devices with their start and end apart: 3, of which 2 were waited for; matrix products, arithmetic and copies ran while one was open for 0% of the time, Pallas kernels for 16%

profile of v2, /device:TPU:16, one launch (start us, length us, event | category | flops | bytes accessed | tf_op | source)
XLA Modules:
  0.0 263.7 jit_solution(9988179418906034098)
XLA Ops:
  6.5 0.1 pad_add_fusion.loader_ref
  6.6 0.9 copy-done.6
  7.6 0.9 copy-done.7
  8.5 0.7 copy-done.9
  9.2 4.9 %pack.1 = (bf16[32,16,1024]{2,1,0:T(8,128)(2,1)S(1)}, bf16[32,16,1024]{2,1,0:T(8,128)(2,1)S(1)}, bf16[32,16,1024]{2,1,0:T(8,128)(2,1)S(1)}, bf16[32,16,1024]{2,1...) custom-call(s32[256]{0:T(256)S(1)} %copy-done.9, s32[3]{0:T(128)S(1)} %pad_add_fusion.loader_ref, ...), custom_call_target="tpu_custom_call" | custom-call | tf_op jit(solution)/shard_map/pack/pallas_call | solution.py:75
  14.1 1.1 copy-done.3
  15.1 1.0 copy-done.4
  16.1 1.5 collective-permute-done
  17.6 0.8 pad_maximum_fusion
  18.5 0.0 all-gather.2.cloned.1.call-update
  18.5 0.0 copy-start.5
  18.5 41.2 %all_to_all.20.refs_0_ = bf16[32,16,1024]{2,1,0:T(8,128)(2,1)S(1)} all-to-all(bf16[32,16,1024]{2,1,0:T(8,128)(2,1)S(1)} %get-tuple-element.14), channel_id=1, replica_groups=mesh['ctx'=16,'head'=2] {'ctx','head'}, dimensions={0} | all-to-all | bytes 2097152 | tf_op jit(solution)/shard_map/all_to_all | solution.py:274
  59.7 48.8 %all_to_all.21.refs_0_ = bf16[32,16,1024]{2,1,0:T(8,128)(2,1)S(1)} all-to-all(bf16[32,16,1024]{2,1,0:T(8,128)(2,1)S(1)} %copy-done.5), channel_id=1, replica_groups=mesh['ctx'=16,'head'=2] {'ctx','head'}, dimensions={0} | all-to-all | bytes 2097152 | tf_op jit(solution)/shard_map/all_to_all | solution.py:274
  108.5 56.6 %all_to_all.22.refs_0_ = bf16[32,16,1024]{2,1,0:T(8,128)(2,1)} all-to-all(bf16[32,16,1024]{2,1,0:T(8,128)(2,1)S(1)} %get-tuple-element.16), channel_id=1, replica_groups=mesh['ctx'=16,'head'=2] {'ctx','head'}, dimensions={0} | all-to-all | bytes 2097152 | tf_op jit(solution)/shard_map/all_to_all | solution.py:274
  165.1 6.3 %all-to-all-start = ((bf16[32,16,1024]{2,1,0:T(8,128)(2,1)}), bf16[32,16,1024]{2,1,0:T(8,128)(2,1)S(1)}, u32[]{:S(2)}, u32[]{:S(2)}) async-start(bf16[32,16,1024]{2,1,0:T(8,128)(2,1)} %copy-done.3), calls=%async_computation | async-start | bytes 2097152 | tf_op jit(solution)/shard_map/all_to_all | solution.py:274
  171.4 0.2 select_reduce_fusion
  171.7 28.9 %all-gather.2.cloned.1.call-done = bf16[4096,1024]{1,0:T(8,128)(2,1)} async-done(((bf16[256,1024]{1,0:T(8,128)(2,1)}), bf16[4096,1024]{1,0:T(8,128)(2,1)}) %all-gather.2.cloned.1.call-update) | async-done | bytes 8388624 | tf_op jit(solution)/shard_map/all_gather | solution.py:272
  200.5 2.9 %window.1 = bf16[144,16,1024]{2,1,0:T(8,128)(2,1)S(1)} custom-call(s32[144]{0:T(256)S(1)} %get-tuple-element.17.rows_ref, bf16[256,16,1024]{2,1,0:T(8,128)(2,1)} %bitcast.14), custom_call_target="tpu_custom_call" | custom-call | bytes 9437184 | tf_op jit(solution)/shard_map/window/pallas_call | solution.py:110
  203.4 12.7 %attend0.1.refs_3_ = bf16[256,4096]{1,0:T(8,128)(2,1)} custom-call(s32[16]{0:T(128)S(1)} %slice.2.slot_ref, s32[4]{0:T(128)S(1)} %copy-done.8, s32[1]{0:T(128)} %bitcast.shard_ref, bf16[32,16,1024]{2,1,0:T(8,128)(2,1)S(1)} %copy-done.2, bf16[2304,1024]{1,0:T(8,128)(2,1)S(1)} %bitcast.6, bf16[2304,1024]{1,0:T(8,128)(2,1)S(1)} %bitcast.7), custom_call_target="tpu_custom_call" | custom-call | flops 2415919104 | bytes 2228224 | tf_op jit(solution)/shard_map/attend0/pallas_call | solution.py:224
  216.2 12.7 %attend1.1.refs_3_ = bf16[256,4096]{1,0:T(8,128)(2,1)} custom-call(s32[16]{0:T(128)S(1)} %slice.2.slot_ref, s32[4]{0:T(128)S(1)} %copy-done.8, s32[1]{0:T(128)} %bitcast.shard_ref, bf16[32,16,1024]{2,1,0:T(8,128)(2,1)S(1)} %all_to_all.21.refs_0_, bf16[2304,1024]{1,0:T(8,128)(2,1)S(1)} %bitcast.8, ...), custom_call_target="tpu_custom_call", output_to_operand_aliasing={{}: (6, {})} | custom-call | flops 2415919104 | bytes 2228224 | tf_op jit(solution)/shard_map/attend1/pallas_call | solution.py:224
  228.9 12.9 %attend2.1.refs_3_ = bf16[256,4096]{1,0:T(8,128)(2,1)} custom-call(s32[16]{0:T(128)S(1)} %slice.2.slot_ref, s32[4]{0:T(128)S(1)} %copy-done.8, s32[1]{0:T(128)} %bitcast.shard_ref, bf16[32,16,1024]{2,1,0:T(8,128)(2,1)S(1)} %all_to_all.20.refs_0_, bf16[2304,1024]{1,0:T(8,128)(2,1)S(1)} %bitcast.10, ...), custom_call_target="tpu_custom_call", output_to_operand_aliasing={{}: (6, {})} | custom-call | flops 2415919104 | bytes 2228224 | tf_op jit(solution)/shard_map/attend2/pallas_call | solution.py:224
  241.8 0.0 all-to-all-done.refs_0_
  241.8 2.3 copy-done.1
  244.2 12.7 %attend3.1 = bf16[256,4096]{1,0:T(8,128)(2,1)} custom-call(s32[16]{0:T(128)S(1)} %slice.2.slot_ref, s32[4]{0:T(128)S(1)} %copy-done.8, s32[1]{0:T(128)} %bitcast.shard_ref, bf16[32,16,1024]{2,1,0:T(8,128)(2,1)S(1)} %all-to-all-done.refs_0_, bf16[2304,1024]{1,0:T(8,128)(2,1)S(1)} %bitcast.12, ...), custom_call_target="tpu_custom_call", output_to_operand_aliasing={{}: (6, {})} | custom-call | flops 2415919104 | bytes 2228224 | tf_op jit(solution)/shard_map/attend3/pallas_call | solution.py:224
  (20 shorter events, 0.1 us)
Async XLA Ops:
  6.5 194.0 %all-gather.2.cloned.1.call-start = ((), (), s32[]{:S(2)}) async-start(), calls=%async_computation.4 | async-start | bytes 8912896 | tf_op jit(solution)/shard_map/all_gather | solution.py:272
  6.6 1.0 copy-start.6
  7.6 0.9 copy-start.7
  8.5 0.7 copy-start.9
  14.1 1.1 copy-start.3
  15.1 1.0 copy-start.4
  16.1 1.5 collective-permute-start
  18.5 41.3 %copy-start.5 = (bf16[32,16,1024]{2,1,0:T(8,128)(2,1)S(1)}, bf16[32,16,1024]{2,1,0:T(8,128)(2,1)}, u32[]{:S(2)}) copy-start(bf16[32,16,1024]{2,1,0:T(8,128)(2,1)} %copy-done.4) | copy-start | bytes 3145732
  108.5 62.9 %copy-start.10 = (s32[256]{0:T(256)S(1)}, s32[256]{0:T(256)}, u32[]{:S(2)}) copy-start(s32[256]{0:T(256)} %place_ref.1) | copy-start | bytes 3076
  165.1 76.7 %all-to-all-start = ((bf16[32,16,1024]{2,1,0:T(8,128)(2,1)}), bf16[32,16,1024]{2,1,0:T(8,128)(2,1)S(1)}, u32[]{:S(2)}, u32[]{:S(2)}) async-start(bf16[32,16,1024]{2,1,0:T(8,128)(2,1)} %copy-done.3), calls=%async_computation | async-start | bytes 2097152 | tf_op jit(solution)/shard_map/all_to_all | solution.py:274
  200.5 2.9 %copy-start.2 = (bf16[32,16,1024]{2,1,0:T(8,128)(2,1)S(1)}, bf16[32,16,1024]{2,1,0:T(8,128)(2,1)}, u32[]{:S(2)}) copy-start(bf16[32,16,1024]{2,1,0:T(8,128)(2,1)} %all_to_all.22.refs_0_) | copy-start | bytes 3145732
  200.5 2.9 %copy-start.8 = (s32[4]{0:T(128)S(1)}, s32[4]{0:T(128)}, u32[]{:S(2)}) copy-start(s32[4]{0:T(128)} %lengths_ref.7) | copy-start | bytes 52
  203.4 25.5 %copy-start = (bf16[144,16,1024]{2,1,0:T(8,128)(2,1)}, bf16[144,16,1024]{2,1,0:T(8,128)(2,1)S(1)}, u32[]{:S(2)}) copy-start(bf16[144,16,1024]{2,1,0:T(8,128)(2,1)S(1)} %window.1) | copy-start | bytes 14155780
  241.8 2.3 copy-start.1
Sparse Core Ops, SparseCore 0:
  18.6 181.8 all-gather.1
